TPU v7x, 512 devices: a whole 4x8x8 slice. The times are simulated.
512 devices in a mesh: kstr: 16 (over y, z_lo), pw: 32 (over x, z_hi, core).
Axes of the slice: x: 4, y: 8, z: 8 (z_hi: 4, z_lo: 2; z = z_hi * 2 + z_lo), core: 2. Of those that a mesh axis runs over, the one named last changes fastest.
Arguments:
- states_re: bfloat16 [16, 256, 16384], P('kstr', None, 'pw'), may hold values from -8 to 8
- states_im: bfloat16 [16, 256, 16384], P('kstr', None, 'pw'), may hold values from -8 to 8
- gmap: int32 [16384], P('pw'), may hold values from 0 to 16383, as said below
Outputs:
- new_re: bfloat16 [16, 256, 16384], P('kstr', None, 'pw')
- new_im: bfloat16 [16, 256, 16384], P('kstr', None, 'pw')
Inputs may be any that keep to these rules, and one draw needn't show every extreme that they name: gmap[G] = (G + o) mod 16384 for one offset o with 1 <= o < 16384.
All inputs are finite; a program needn't handle non-finite values.
Results may differ from a plain program's by a relative error of at most 0.008.
Values may be sent and summed in bfloat16 or wider, within the bound.
No kernel may reach another device: no remote copies, remote signals or barrier semaphores. Data moves between devices by JAX's collectives and lax.ppermute only.
A program may use at most 64 MiB of HBM per device.

v0:
```python
import jax
import jax.numpy as jnp
from jax import lax
from jax.sharding import PartitionSpec as P

NEWTON = 4
STEPS = 2
HIGH = lax.Precision.HIGHEST
EPS_SCALE = 1e-06
EPS_NORM = 1e-06
TAU_STEP = 0.25


def shifted(value, axis, by):
    count = lax.axis_size(axis)
    return lax.ppermute(value, axis, [(i, (i + by) % count) for i in range(count)])


def complex_mul(left, right):

    def matmul(first, second):
        return jnp.einsum("kij,kjl->kil", first, second, precision=HIGH)

    real = matmul(left[:, 0], right[:, 0]) - matmul(left[:, 1], right[:, 1])
    imag = matmul(left[:, 0], right[:, 1]) + matmul(left[:, 1], right[:, 0])
    return jnp.stack([real, imag], 1)


def start_inverse(whole):
    magnitude = jnp.sqrt(whole[:, 0] * whole[:, 0] + whole[:, 1] * whole[:, 1])
    colmax = jnp.max(jnp.sum(magnitude, axis=1), axis=1)
    rowmax = jnp.max(jnp.sum(magnitude, axis=2), axis=1)
    factor = (1.0 / (colmax * rowmax + EPS_SCALE))[:, None, None]
    return jnp.stack(
        [jnp.swapaxes(whole[:, 0], 1, 2) * factor, -jnp.swapaxes(whole[:, 1], 1, 2) * factor], 1
    )


def newton_full(whole):
    iterate = start_inverse(whole)
    for turn in range(NEWTON):
        iterate = 2.0 * iterate - complex_mul(iterate, complex_mul(whole, iterate))
    return iterate


def bf_product(form, left, right):
    return jnp.einsum(form, left, right, preferred_element_type=jnp.float32)


def dual_terms(rounded, states):
    real = bf_product("kmn,kmg->kng", rounded[:, 0], states[:, 0]) + bf_product(
        "kmn,kmg->kng", rounded[:, 1], states[:, 1]
    )
    imag = bf_product("kmn,kmg->kng", rounded[:, 0], states[:, 1]) - bf_product(
        "kmn,kmg->kng", rounded[:, 1], states[:, 0]
    )
    return jnp.stack([real, imag], 1).astype(jnp.bfloat16)


def rotate_columns(block, amount, width):
    blocks_off = amount // width
    rest = amount % width
    plane_size = lax.axis_size("pw")
    for bit in range((plane_size - 1).bit_length()):
        moved = shifted(block, "pw", -(1 << bit))
        block = jnp.where(jnp.bitwise_and(jnp.right_shift(blocks_off, bit), 1) == 1, moved, block)
    after = shifted(block, "pw", -1)
    joined = jnp.concatenate([block, after], block.ndim - 1)
    return lax.dynamic_slice_in_dim(joined, rest, width, block.ndim - 1)


def body(states_re, states_im, gmap):
    kpoints, bands, width = states_re.shape
    string_size = lax.axis_size("kstr")
    plane_size = lax.axis_size("pw")
    string_index = lax.axis_index("kstr")
    total_width = width * plane_size
    offset = jnp.mod(gmap[0] - lax.axis_index("pw") * width, total_width)
    back_offset = jnp.mod(total_width - offset, total_width)
    at_first = string_index == 0
    at_last = string_index == string_size - 1
    count_all = 2 * kpoints * string_size * bands * width * plane_size
    states = jnp.stack([states_re, states_im], 1)
    for step in range(STEPS):
        ahead = shifted(states, "kstr", -1)
        turned = rotate_columns(ahead, offset, width)
        ahead = jnp.where(at_last, turned, ahead)
        following = jnp.concatenate([states[1:], ahead], 0)
        s_re = bf_product("kmg,kng->kmn", states[:, 0], following[:, 0]) + bf_product(
            "kmg,kng->kmn", states[:, 1], following[:, 1]
        )
        s_im = bf_product("kmg,kng->kmn", states[:, 0], following[:, 1]) - bf_product(
            "kmg,kng->kmn", states[:, 1], following[:, 0]
        )
        partial_value = jnp.stack([s_re, s_im], 1)
        whole = lax.psum(partial_value, "pw") / (width * plane_size)
        inverse = newton_full(whole)
        rounded = inverse.astype(jnp.bfloat16)
        a_re = bf_product("kmn,kmg->kng", rounded[:, 0], following[:, 0]) - bf_product(
            "kmn,kmg->kng", rounded[:, 1], following[:, 1]
        )
        a_im = bf_product("kmn,kmg->kng", rounded[:, 0], following[:, 1]) + bf_product(
            "kmn,kmg->kng", rounded[:, 1], following[:, 0]
        )
        local_terms = dual_terms(rounded, states)
        arrived = shifted(local_terms, "kstr", 1)
        earlier = local_terms[:-1]
        placed = rotate_columns(arrived, back_offset, width)
        arrived = jnp.where(at_first, placed, arrived)
        incoming = jnp.concatenate([arrived, earlier], 0).astype(jnp.float32)
        g_re = a_im - incoming[:, 1]
        g_im = incoming[:, 0] - a_re
        total = lax.psum(jnp.sum(g_re * g_re + g_im * g_im), ("kstr", "pw"))
        rms = jnp.sqrt(total / count_all + EPS_NORM)
        new_re = (states[:, 0].astype(jnp.float32) + TAU_STEP * g_re / rms).astype(jnp.bfloat16)
        new_im = (states[:, 1].astype(jnp.float32) + TAU_STEP * g_im / rms).astype(jnp.bfloat16)
        states = jnp.stack([new_re, new_im], 1)
    return (states[:, 0], states[:, 1])


def solution(mesh):
    placed = (P("kstr", None, "pw"), P("kstr", None, "pw"), P("pw"))
    return jax.shard_map(
        body,
        mesh=mesh,
        in_specs=placed,
        out_specs=(P("kstr", None, "pw"), P("kstr", None, "pw")),
        check_vma=False,
    )
```

profile of v0, /device:TPU:25, one launch (start us, length us, event | category | flops | bytes accessed | tf_op | source)
XLA Modules:
  0.0 1402.9 jit_solution(1617140451742188734)
XLA Ops:
  7.2 1.1 pad_maximum_fusion
  8.3 3.9 collective-permute-start
  12.2 11.7 collective-permute-done
  23.9 3.1 collective-permute-start.1
  27.1 1.2 slice.58
  29.0 9.8 collective-permute-done.1
  38.8 17.5 %collective-permute-start.2 = (bf16[1,2,256,512]{3,2,1,0:T(8,128)(2,1)S(1)}, bf16[1,2,256,512]{3,2,1,0:T(8,128)(2,1)S(1)}, u32[]{:S(2)}, u32[]{:S(2)}) collective-permute-start(bf16[1,2,256,512]{3,2,1,0:T(8,128)(2,1)S(1)} %broadcast_select_fusion.11), channel_id=1, source_target_pairs={{0,30},{1,31},{2,0},{3,1},{4,2},{5,3},{6,4},{7,5},{8,6},{9,7},{10,... | collective-permute-start | bytes 1572872 | tf_op jit(solution)/shard_map/ppermute | solution.py:16
  56.3 17.4 %collective-permute-done.2 = bf16[1,2,256,512]{3,2,1,0:T(8,128)(2,1)S(1)} collective-permute-done((bf16[1,2,256,512]{3,2,1,0:T(8,128)(2,1)S(1)}, bf16[1,2,256,512]{3,2,1,0:T(8,128)(2,1)S(1)}, u32[]{:S(2)}, u32[]{:S(2)}) %collective-permute-start.2) | collective-permute-done | bytes 524320 | tf_op jit(solution)/shard_map/ppermute | solution.py:16
  73.7 1.9 collective-permute-start.3
  75.7 15.9 %collective-permute-done.3 = bf16[1,2,256,512]{3,2,1,0:T(8,128)(2,1)S(1)} collective-permute-done((bf16[1,2,256,512]{3,2,1,0:T(8,128)(2,1)S(1)}, bf16[1,2,256,512]{3,2,1,0:T(8,128)(2,1)S(1)}, u32[]{:S(2)}, u32[]{:S(2)}) %collective-permute-start.3) | collective-permute-done | bytes 524320 | tf_op jit(solution)/shard_map/ppermute | solution.py:16
  91.6 1.9 collective-permute-start.4
  93.6 12.9 collective-permute-done.4
  106.6 1.9 collective-permute-start.5
  108.5 15.0 %collective-permute-done.5 = bf16[1,2,256,512]{3,2,1,0:T(8,128)(2,1)S(1)} collective-permute-done((bf16[1,2,256,512]{3,2,1,0:T(8,128)(2,1)S(1)}, bf16[1,2,256,512]{3,2,1,0:T(8,128)(2,1)S(1)}, u32[]{:S(2)}, u32[]{:S(2)}) %collective-permute-start.5) | collective-permute-done | bytes 524320 | tf_op jit(solution)/shard_map/ppermute | solution.py:16
  123.5 2.7 collective-permute-start.6
  126.3 24.4 %collective-permute-done.6 = bf16[1,2,256,512]{3,2,1,0:T(8,128)(2,1)S(1)} collective-permute-done((bf16[1,2,256,512]{3,2,1,0:T(8,128)(2,1)S(1)}, bf16[1,2,256,512]{3,2,1,0:T(8,128)(2,1)S(1)}, u32[]{:S(2)}, u32[]{:S(2)}) %collective-permute-start.6) | collective-permute-done | bytes 524320 | tf_op jit(solution)/shard_map/ppermute | solution.py:16
  154.1 290.5 %all-reduce.3.cloned.1.call-done = f32[1,2,256,256]{2,3,1,0:T(8,128)} async-done(((f32[1,2,256,256]{2,3,1,0:T(8,128)}), f32[1,2,256,256]{2,3,1,0:T(8,128)}) %all-reduce.3.cloned.1.call-update) | async-done | bytes 524304 | tf_op jit(solution)/shard_map/psum | solution.py:96
  444.6 1.1 broadcast_multiply_fusion.1
  466.1 2.4 collective-permute-start.7
  468.5 13.5 collective-permute-done.7
  482.1 3.1 collective-permute-start.8
  485.2 13.9 collective-permute-done.8
  499.1 7.2 collective-permute-start.9
  506.3 19.8 %collective-permute-done.9 = bf16[1,2,256,512]{3,2,1,0:T(8,128)(2,1)S(1)} collective-permute-done((bf16[1,2,256,512]{3,2,1,0:T(8,128)(2,1)S(1)}, bf16[1,2,256,512]{3,2,1,0:T(8,128)(2,1)S(1)}, u32[]{:S(2)}, u32[]{:S(2)}) %collective-permute-start.9) | collective-permute-done | bytes 524320 | tf_op jit(solution)/shard_map/ppermute | solution.py:16
  526.2 1.9 collective-permute-start.10
  528.1 24.4 %collective-permute-done.10 = bf16[1,2,256,512]{3,2,1,0:T(8,128)(2,1)S(1)} collective-permute-done((bf16[1,2,256,512]{3,2,1,0:T(8,128)(2,1)S(1)}, bf16[1,2,256,512]{3,2,1,0:T(8,128)(2,1)S(1)}, u32[]{:S(2)}, u32[]{:S(2)}) %collective-permute-start.10) | collective-permute-done | bytes 524320 | tf_op jit(solution)/shard_map/ppermute | solution.py:16
  552.6 1.9 collective-permute-start.11
  554.5 8.0 collective-permute-done.11
  562.6 1.9 collective-permute-start.12
  564.5 9.5 collective-permute-done.12
  574.1 10.1 collective-permute-start.13
  585.0 15.4 %collective-permute-done.13 = bf16[1,2,256,512]{3,2,1,0:T(8,128)(2,1)S(1)} collective-permute-done((bf16[1,2,256,512]{3,2,1,0:T(8,128)(2,1)S(1)}, bf16[1,2,256,512]{3,2,1,0:T(8,128)(2,1)S(1)}, u32[]{:S(2)}, u32[]{:S(2)}) %collective-permute-start.13) | collective-permute-done | bytes 524320 | tf_op jit(solution)/shard_map/ppermute | solution.py:16
  601.8 100.3 %psum.29 = f32[]{:T(128)} all-reduce(f32[]{:T(128)} %get-tuple-element.10), channel_id=1, replica_groups=mesh['kstr'=16,'pw'=32] {'kstr','pw'}, use_global_device_ids=true, to_apply=%region_6.7 | all-reduce | flops 1 | bytes 8 | tf_op jit(solution)/shard_map/psum | solution.py:113
  703.1 1.9 collective-permute-start.14
  705.1 13.2 collective-permute-done.14
  718.3 3.0 collective-permute-start.15
  721.3 10.5 collective-permute-done.15
  731.8 6.3 collective-permute-start.16
  738.2 9.4 collective-permute-done.16
  747.6 5.2 collective-permute-start.17
  752.8 19.0 %collective-permute-done.17 = bf16[1,2,256,512]{3,2,1,0:T(8,128)(2,1)S(1)} collective-permute-done((bf16[1,2,256,512]{3,2,1,0:T(8,128)(2,1)S(1)}, bf16[1,2,256,512]{3,2,1,0:T(8,128)(2,1)S(1)}, u32[]{:S(2)}, u32[]{:S(2)}) %collective-permute-start.17) | collective-permute-done | bytes 524320 | tf_op jit(solution)/shard_map/ppermute | solution.py:16
  771.9 2.5 collective-permute-start.18
  774.4 12.0 collective-permute-done.18
  786.4 7.7 collective-permute-start.19
  794.2 10.7 collective-permute-done.19
  804.9 4.5 collective-permute-start.20
  809.4 12.8 collective-permute-done.20
  824.6 311.5 %all-reduce.5.cloned.1.call-done = f32[1,2,256,256]{2,3,1,0:T(8,128)} async-done(((f32[1,2,256,256]{2,3,1,0:T(8,128)}), f32[1,2,256,256]{2,3,1,0:T(8,128)}) %all-reduce.5.cloned.1.call-update) | async-done | bytes 524304 | tf_op jit(solution)/shard_map/psum | solution.py:96
  1136.1 1.1 broadcast_multiply_fusion
  1157.6 2.4 collective-permute-start.21
  1160.1 13.5 collective-permute-done.21
  1173.6 3.1 collective-permute-start.22
  1176.7 13.9 collective-permute-done.22
  1190.6 7.2 collective-permute-start.23
  1197.8 19.8 %collective-permute-done.23 = bf16[1,2,256,512]{3,2,1,0:T(8,128)(2,1)S(1)} collective-permute-done((bf16[1,2,256,512]{3,2,1,0:T(8,128)(2,1)S(1)}, bf16[1,2,256,512]{3,2,1,0:T(8,128)(2,1)S(1)}, u32[]{:S(2)}, u32[]{:S(2)}) %collective-permute-start.23) | collective-permute-done | bytes 524320 | tf_op jit(solution)/shard_map/ppermute | solution.py:16
  1217.7 1.9 collective-permute-start.24
  1219.6 24.3 %collective-permute-done.24 = bf16[1,2,256,512]{3,2,1,0:T(8,128)(2,1)S(1)} collective-permute-done((bf16[1,2,256,512]{3,2,1,0:T(8,128)(2,1)S(1)}, bf16[1,2,256,512]{3,2,1,0:T(8,128)(2,1)S(1)}, u32[]{:S(2)}, u32[]{:S(2)}) %collective-permute-start.24) | collective-permute-done | bytes 524320 | tf_op jit(solution)/shard_map/ppermute | solution.py:16
  1244.0 1.9 collective-permute-start.25
  1245.9 8.0 collective-permute-done.25
  1254.0 1.9 collective-permute-start.26
  1255.9 9.5 collective-permute-done.26
  1265.5 10.7 collective-permute-start.27
  1276.9 14.9 %collective-permute-done.27 = bf16[1,2,256,512]{3,2,1,0:T(8,128)(2,1)S(1)} collective-permute-done((bf16[1,2,256,512]{3,2,1,0:T(8,128)(2,1)S(1)}, bf16[1,2,256,512]{3,2,1,0:T(8,128)(2,1)S(1)}, u32[]{:S(2)}, u32[]{:S(2)}) %collective-permute-start.27) | collective-permute-done | bytes 524320 | tf_op jit(solution)/shard_map/ppermute | solution.py:16
  1293.3 100.3 %psum.31 = f32[]{:T(128)} all-reduce(f32[]{:T(128)} %get-tuple-element.12), channel_id=1, replica_groups=mesh['kstr'=16,'pw'=32] {'kstr','pw'}, use_global_device_ids=true, to_apply=%region_13.14 | all-reduce | flops 1 | bytes 8 | tf_op jit(solution)/shard_map/psum | solution.py:113
  (144 shorter events, 50.8 us)
Async XLA Ops:
  7.2 437.4 %all-reduce.3.cloned.1.call-start = ((), (), s32[]{:S(2)}) async-start(), calls=%async_computation | async-start | bytes 1048576 | tf_op jit(solution)/shard_map/psum | solution.py:96
  8.3 15.6 %collective-permute-start = (bf16[1,2,256,512]{3,2,1,0:T(8,128)(2,1)S(1)}, bf16[1,2,256,512]{3,2,1,0:T(8,128)(2,1)S(1)}, u32[]{:S(2)}, u32[]{:S(2)}) collective-permute-start(bf16[1,2,256,512]{3,2,1,0:T(8,128)(2,1)S(1)} %pad_maximum_fusion), channel_id=1, source_target_pairs={{0,480},{32,0},{64,32},{96,64},{128,96},{160,128},{192,160},{224,1... | collective-permute-start | bytes 1572872 | tf_op jit(solution)/shard_map/ppermute | solution.py:16
  23.9 14.8 %collective-permute-start.1 = (bf16[1,2,256,512]{3,2,1,0:T(8,128)(2,1)S(1)}, bf16[1,2,256,512]{3,2,1,0:T(8,128)(2,1)S(1)}, u32[]{:S(2)}, u32[]{:S(2)}) collective-permute-start(bf16[1,2,256,512]{3,2,1,0:T(8,128)(2,1)S(1)} %collective-permute-done), channel_id=1, source_target_pairs={{0,31},{1,0},{2,1},{3,2},{4,3},{5,4},{6,5},{7,6},{8,7},{9,8},{10,9... | collective-permute-start | bytes 1572872 | tf_op jit(solution)/shard_map/ppermute | solution.py:16
  38.8 34.9 %collective-permute-start.2 = (bf16[1,2,256,512]{3,2,1,0:T(8,128)(2,1)S(1)}, bf16[1,2,256,512]{3,2,1,0:T(8,128)(2,1)S(1)}, u32[]{:S(2)}, u32[]{:S(2)}) collective-permute-start(bf16[1,2,256,512]{3,2,1,0:T(8,128)(2,1)S(1)} %broadcast_select_fusion.11), channel_id=1, source_target_pairs={{0,30},{1,31},{2,0},{3,1},{4,2},{5,3},{6,4},{7,5},{8,6},{9,7},{10,... | collective-permute-start | bytes 1572872 | tf_op jit(solution)/shard_map/ppermute | solution.py:16
  73.7 17.8 %collective-permute-start.3 = (bf16[1,2,256,512]{3,2,1,0:T(8,128)(2,1)S(1)}, bf16[1,2,256,512]{3,2,1,0:T(8,128)(2,1)S(1)}, u32[]{:S(2)}, u32[]{:S(2)}) collective-permute-start(bf16[1,2,256,512]{3,2,1,0:T(8,128)(2,1)S(1)} %broadcast_select_fusion.13), channel_id=1, source_target_pairs={{0,28},{1,29},{2,30},{3,31},{4,0},{5,1},{6,2},{7,3},{8,4},{9,5},{1... | collective-permute-start | bytes 1572872 | tf_op jit(solution)/shard_map/ppermute | solution.py:16
  91.6 14.9 %collective-permute-start.4 = (bf16[1,2,256,512]{3,2,1,0:T(8,128)(2,1)S(1)}, bf16[1,2,256,512]{3,2,1,0:T(8,128)(2,1)S(1)}, u32[]{:S(2)}, u32[]{:S(2)}) collective-permute-start(bf16[1,2,256,512]{3,2,1,0:T(8,128)(2,1)S(1)} %broadcast_select_fusion.15), channel_id=1, source_target_pairs={{0,24},{1,25},{2,26},{3,27},{4,28},{5,29},{6,30},{7,31},{8,0},{9,1... | collective-permute-start | bytes 1572872 | tf_op jit(solution)/shard_map/ppermute | solution.py:16
  106.6 16.9 %collective-permute-start.5 = (bf16[1,2,256,512]{3,2,1,0:T(8,128)(2,1)S(1)}, bf16[1,2,256,512]{3,2,1,0:T(8,128)(2,1)S(1)}, u32[]{:S(2)}, u32[]{:S(2)}) collective-permute-start(bf16[1,2,256,512]{3,2,1,0:T(8,128)(2,1)S(1)} %broadcast_select_fusion.17), channel_id=1, source_target_pairs={{0,16},{1,17},{2,18},{3,19},{4,20},{5,21},{6,22},{7,23},{8,24},{9,... | collective-permute-start | bytes 1572872 | tf_op jit(solution)/shard_map/ppermute | solution.py:16
  123.5 27.2 %collective-permute-start.6 = (bf16[1,2,256,512]{3,2,1,0:T(8,128)(2,1)S(1)}, bf16[1,2,256,512]{3,2,1,0:T(8,128)(2,1)S(1)}, u32[]{:S(2)}, u32[]{:S(2)}) collective-permute-start(bf16[1,2,256,512]{3,2,1,0:T(8,128)(2,1)S(1)} %broadcast_select_fusion.19), channel_id=1, source_target_pairs={{0,31},{1,0},{2,1},{3,2},{4,3},{5,4},{6,5},{7,6},{8,7},{9,8},{10,9... | collective-permute-start | bytes 1572872 | tf_op jit(solution)/shard_map/ppermute | solution.py:16
  126.3 24.9 %copy-start = (bf16[1,256,512]{2,1,0:T(8,128)(2,1)S(1)}, bf16[1,256,512]{2,1,0:T(8,128)(2,1)}, u32[]{:S(2)}) copy-start(bf16[1,256,512]{2,1,0:T(8,128)(2,1)} %param.4) | copy-start | bytes 786436
  151.5 1.0 copy-start.1
  153.8 982.2 %all-reduce.5.cloned.1.call-start = ((), (), s32[]{:S(2)}) async-start(), calls=%async_computation.1 | async-start | bytes 1048576 | tf_op jit(solution)/shard_map/psum | solution.py:96
  466.1 15.9 %collective-permute-start.7 = (bf16[1,2,256,512]{3,2,1,0:T(8,128)(2,1)S(1)}, bf16[1,2,256,512]{3,2,1,0:T(8,128)(2,1)S(1)}, u32[]{:S(2)}, u32[]{:S(2)}) collective-permute-start(bf16[1,2,256,512]{3,2,1,0:T(8,128)(2,1)S(1)} %pad_maximum_fusion.2), channel_id=1, source_target_pairs={{0,32},{32,64},{64,96},{96,128},{128,160},{160,192},{192,224},{224... | collective-permute-start | bytes 1572872 | tf_op jit(solution)/shard_map/ppermute | solution.py:16
  482.1 17.0 %collective-permute-start.8 = (bf16[1,2,256,512]{3,2,1,0:T(8,128)(2,1)S(1)}, bf16[1,2,256,512]{3,2,1,0:T(8,128)(2,1)S(1)}, u32[]{:S(2)}, u32[]{:S(2)}) collective-permute-start(bf16[1,2,256,512]{3,2,1,0:T(8,128)(2,1)S(1)} %collective-permute-done.7), channel_id=1, source_target_pairs={{0,31},{1,0},{2,1},{3,2},{4,3},{5,4},{6,5},{7,6},{8,7},{9,8},{10,9... | collective-permute-start | bytes 1572872 | tf_op jit(solution)/shard_map/ppermute | solution.py:16
  499.1 27.0 %collective-permute-start.9 = (bf16[1,2,256,512]{3,2,1,0:T(8,128)(2,1)S(1)}, bf16[1,2,256,512]{3,2,1,0:T(8,128)(2,1)S(1)}, u32[]{:S(2)}, u32[]{:S(2)}) collective-permute-start(bf16[1,2,256,512]{3,2,1,0:T(8,128)(2,1)S(1)} %broadcast_select_fusion.1), channel_id=1, source_target_pairs={{0,30},{1,31},{2,0},{3,1},{4,2},{5,3},{6,4},{7,5},{8,6},{9,7},{10,... | collective-permute-start | bytes 1572872 | tf_op jit(solution)/shard_map/ppermute | solution.py:16
  526.2 26.3 %collective-permute-start.10 = (bf16[1,2,256,512]{3,2,1,0:T(8,128)(2,1)S(1)}, bf16[1,2,256,512]{3,2,1,0:T(8,128)(2,1)S(1)}, u32[]{:S(2)}, u32[]{:S(2)}) collective-permute-start(bf16[1,2,256,512]{3,2,1,0:T(8,128)(2,1)S(1)} %broadcast_select_fusion.3), channel_id=1, source_target_pairs={{0,28},{1,29},{2,30},{3,31},{4,0},{5,1},{6,2},{7,3},{8,4},{9,5},{1... | collective-permute-start | bytes 1572872 | tf_op jit(solution)/shard_map/ppermute | solution.py:16
  552.6 9.9 collective-permute-start.11
  562.6 11.4 collective-permute-start.12
  574.1 26.2 %collective-permute-start.13 = (bf16[1,2,256,512]{3,2,1,0:T(8,128)(2,1)S(1)}, bf16[1,2,256,512]{3,2,1,0:T(8,128)(2,1)S(1)}, u32[]{:S(2)}, u32[]{:S(2)}) collective-permute-start(bf16[1,2,256,512]{3,2,1,0:T(8,128)(2,1)S(1)} %broadcast_select_fusion.9), channel_id=1, source_target_pairs={{0,31},{1,0},{2,1},{3,2},{4,3},{5,4},{6,5},{7,6},{8,7},{9,8},{10,9... | collective-permute-start | bytes 1572872 | tf_op jit(solution)/shard_map/ppermute | solution.py:16
  703.1 15.2 %collective-permute-start.14 = (bf16[1,2,256,512]{3,2,1,0:T(8,128)(2,1)S(1)}, bf16[1,2,256,512]{3,2,1,0:T(8,128)(2,1)S(1)}, u32[]{:S(2)}, u32[]{:S(2)}) collective-permute-start(bf16[1,2,256,512]{3,2,1,0:T(8,128)(2,1)S(1)} %pad_maximum_fusion.3), channel_id=1, source_target_pairs={{0,480},{32,0},{64,32},{96,64},{128,96},{160,128},{192,160},{224,1... | collective-permute-start | bytes 1572872 | tf_op jit(solution)/shard_map/ppermute | solution.py:16
  718.3 13.5 collective-permute-start.15
  731.8 15.7 %collective-permute-start.16 = (bf16[1,2,256,512]{3,2,1,0:T(8,128)(2,1)S(1)}, bf16[1,2,256,512]{3,2,1,0:T(8,128)(2,1)S(1)}, u32[]{:S(2)}, u32[]{:S(2)}) collective-permute-start(bf16[1,2,256,512]{3,2,1,0:T(8,128)(2,1)S(1)} %broadcast_select_fusion.10), channel_id=1, source_target_pairs={{0,30},{1,31},{2,0},{3,1},{4,2},{5,3},{6,4},{7,5},{8,6},{9,7},{10,... | collective-permute-start | bytes 1572872 | tf_op jit(solution)/shard_map/ppermute | solution.py:16
  747.6 24.2 %collective-permute-start.17 = (bf16[1,2,256,512]{3,2,1,0:T(8,128)(2,1)S(1)}, bf16[1,2,256,512]{3,2,1,0:T(8,128)(2,1)S(1)}, u32[]{:S(2)}, u32[]{:S(2)}) collective-permute-start(bf16[1,2,256,512]{3,2,1,0:T(8,128)(2,1)S(1)} %broadcast_select_fusion.12), channel_id=1, source_target_pairs={{0,28},{1,29},{2,30},{3,31},{4,0},{5,1},{6,2},{7,3},{8,4},{9,5},{1... | collective-permute-start | bytes 1572872 | tf_op jit(solution)/shard_map/ppermute | solution.py:16
  771.9 14.5 %collective-permute-start.18 = (bf16[1,2,256,512]{3,2,1,0:T(8,128)(2,1)S(1)}, bf16[1,2,256,512]{3,2,1,0:T(8,128)(2,1)S(1)}, u32[]{:S(2)}, u32[]{:S(2)}) collective-permute-start(bf16[1,2,256,512]{3,2,1,0:T(8,128)(2,1)S(1)} %broadcast_select_fusion.14), channel_id=1, source_target_pairs={{0,24},{1,25},{2,26},{3,27},{4,28},{5,29},{6,30},{7,31},{8,0},{9,1... | collective-permute-start | bytes 1572872 | tf_op jit(solution)/shard_map/ppermute | solution.py:16
  786.4 18.4 %collective-permute-start.19 = (bf16[1,2,256,512]{3,2,1,0:T(8,128)(2,1)S(1)}, bf16[1,2,256,512]{3,2,1,0:T(8,128)(2,1)S(1)}, u32[]{:S(2)}, u32[]{:S(2)}) collective-permute-start(bf16[1,2,256,512]{3,2,1,0:T(8,128)(2,1)S(1)} %broadcast_select_fusion.16), channel_id=1, source_target_pairs={{0,16},{1,17},{2,18},{3,19},{4,20},{5,21},{6,22},{7,23},{8,24},{9,... | collective-permute-start | bytes 1572872 | tf_op jit(solution)/shard_map/ppermute | solution.py:16
  804.9 17.3 %collective-permute-start.20 = (bf16[1,2,256,512]{3,2,1,0:T(8,128)(2,1)S(1)}, bf16[1,2,256,512]{3,2,1,0:T(8,128)(2,1)S(1)}, u32[]{:S(2)}, u32[]{:S(2)}) collective-permute-start(bf16[1,2,256,512]{3,2,1,0:T(8,128)(2,1)S(1)} %broadcast_select_fusion.18), channel_id=1, source_target_pairs={{0,31},{1,0},{2,1},{3,2},{4,3},{5,4},{6,5},{7,6},{8,7},{9,8},{10,9... | collective-permute-start | bytes 1572872 | tf_op jit(solution)/shard_map/ppermute | solution.py:16
  1157.6 15.9 %collective-permute-start.21 = (bf16[1,2,256,512]{3,2,1,0:T(8,128)(2,1)S(1)}, bf16[1,2,256,512]{3,2,1,0:T(8,128)(2,1)S(1)}, u32[]{:S(2)}, u32[]{:S(2)}) collective-permute-start(bf16[1,2,256,512]{3,2,1,0:T(8,128)(2,1)S(1)} %pad_maximum_fusion.5), channel_id=1, source_target_pairs={{0,32},{32,64},{64,96},{96,128},{128,160},{160,192},{192,224},{224... | collective-permute-start | bytes 1572872 | tf_op jit(solution)/shard_map/ppermute | solution.py:16
  1173.6 17.0 %collective-permute-start.22 = (bf16[1,2,256,512]{3,2,1,0:T(8,128)(2,1)S(1)}, bf16[1,2,256,512]{3,2,1,0:T(8,128)(2,1)S(1)}, u32[]{:S(2)}, u32[]{:S(2)}) collective-permute-start(bf16[1,2,256,512]{3,2,1,0:T(8,128)(2,1)S(1)} %collective-permute-done.21), channel_id=1, source_target_pairs={{0,31},{1,0},{2,1},{3,2},{4,3},{5,4},{6,5},{7,6},{8,7},{9,8},{10,9... | collective-permute-start | bytes 1572872 | tf_op jit(solution)/shard_map/ppermute | solution.py:16
  1190.6 27.0 %collective-permute-start.23 = (bf16[1,2,256,512]{3,2,1,0:T(8,128)(2,1)S(1)}, bf16[1,2,256,512]{3,2,1,0:T(8,128)(2,1)S(1)}, u32[]{:S(2)}, u32[]{:S(2)}) collective-permute-start(bf16[1,2,256,512]{3,2,1,0:T(8,128)(2,1)S(1)} %broadcast_select_fusion), channel_id=1, source_target_pairs={{0,30},{1,31},{2,0},{3,1},{4,2},{5,3},{6,4},{7,5},{8,6},{9,7},{10,... | collective-permute-start | bytes 1572872 | tf_op jit(solution)/shard_map/ppermute | solution.py:16
  1217.7 26.2 %collective-permute-start.24 = (bf16[1,2,256,512]{3,2,1,0:T(8,128)(2,1)S(1)}, bf16[1,2,256,512]{3,2,1,0:T(8,128)(2,1)S(1)}, u32[]{:S(2)}, u32[]{:S(2)}) collective-permute-start(bf16[1,2,256,512]{3,2,1,0:T(8,128)(2,1)S(1)} %broadcast_select_fusion.2), channel_id=1, source_target_pairs={{0,28},{1,29},{2,30},{3,31},{4,0},{5,1},{6,2},{7,3},{8,4},{9,5},{1... | collective-permute-start | bytes 1572872 | tf_op jit(solution)/shard_map/ppermute | solution.py:16
  1244.0 9.9 collective-permute-start.25
  1254.0 11.4 collective-permute-start.26
  1265.5 26.3 %collective-permute-start.27 = (bf16[1,2,256,512]{3,2,1,0:T(8,128)(2,1)S(1)}, bf16[1,2,256,512]{3,2,1,0:T(8,128)(2,1)S(1)}, u32[]{:S(2)}, u32[]{:S(2)}) collective-permute-start(bf16[1,2,256,512]{3,2,1,0:T(8,128)(2,1)S(1)} %broadcast_select_fusion.8), channel_id=1, source_target_pairs={{0,31},{1,0},{2,1},{3,2},{4,3},{5,4},{6,5},{7,6},{8,7},{9,8},{10,9... | collective-permute-start | bytes 1572872 | tf_op jit(solution)/shard_map/ppermute | solution.py:16
Sparse Core Ops, SparseCore 0:
  154.0 290.5 all-reduce.2
  824.7 311.3 all-reduce.4
where the time goes:
time: 1410 us; the launch traced here: 1400 us
  waiting for transfers between devices  1010 us (72%)
  blocking collectives  201 us (14%)
  starting transfers between devices  122 us (9%)
  matrix products  38.8 us (3%)
  between operations  20.2 us (1%)
  other arithmetic  14.2 us (1%)
    psum x2, waiting for transfers between devices, body(): whole = lax.psum(partial_value, 'pw') / (width * plane_size)  602 us
    ppermute x28, waiting for transfers between devices, shifted(): lax.ppermute(value, axis, [(i, (i + by) % count) for i in range(count)])  403 us
    psum x2, blocking collectives, body(): total = lax.psum(jnp.sum(g_re * g_re + g_im * g_im), ('kstr', 'pw'))  201 us
    ppermute x28, starting transfers between devices, shifted(): lax.ppermute(value, axis, [(i, (i + by) % count) for i in range(count)])  122 us
    dot_general x64, matrix products, matmul(): return jnp.einsum('kij,kjl->kil', first, second, precision=HIGH)  31.5 us
  transfers between devices with their start and end apart: 30, of which 30 were waited for; matrix products, arithmetic and copies ran while one was open for 0% of the time, Pallas kernels for 0%

commit v1 on v0

--- a/solution.py
+++ b/solution.py
@@ -93,7 +93,7 @@
             "kmg,kng->kmn", states[:, 1], following[:, 0]
         )
         partial_value = jnp.stack([s_re, s_im], 1)
-        whole = lax.psum(partial_value, "pw") / (width * plane_size)
+        whole = jnp.sum(lax.all_gather(partial_value, "pw"), axis=0) / (width * plane_size)
         inverse = newton_full(whole)
         rounded = inverse.astype(jnp.bfloat16)
         a_re = bf_product("kmn,kmg->kng", rounded[:, 0], following[:, 0]) - bf_product(

time: 1410 us -> 1100 us (0.78)
  the two profiles are of different devices: /device:TPU:25 before, /device:TPU:1 now
where the time goes in v1:
time: 1100 us; the launch traced here: 1090 us
  waiting for transfers between devices  661 us (60%)
  blocking collectives  210 us (19%)
  starting transfers between devices  134 us (12%)
  matrix products  42.8 us (4%)
  other arithmetic  24.9 us (2%)
  between operations  20.3 us (2%)
    ppermute x28, waiting for transfers between devices, shifted(): lax.ppermute(value, axis, [(i, (i + by) % count) for i in range(count)])  391 us
    all_gather x2, waiting for transfers between devices, body(): lax.all_gather(partial_value, 'pw')  270 us
    psum x2, blocking collectives, body(): total = lax.psum(jnp.sum(g_re * g_re + g_im * g_im), ('kstr', 'pw'))  210 us
    ppermute x28, starting transfers between devices, shifted(): lax.ppermute(value, axis, [(i, (i + by) % count) for i in range(count)])  134 us
    dot_general x64, matrix products, matmul(): return jnp.einsum('kij,kjl->kil', first, second, precision=HIGH)  31.7 us
  transfers between devices with their start and end apart: 30, of which 30 were waited for; matrix products, arithmetic and copies ran while one was open for 0% of the time, Pallas kernels for 0%

profile of v1, /device:TPU:1, one launch (start us, length us, event | category | flops | bytes accessed | tf_op | source)
XLA Modules:
  0.0 1094.6 jit_solution(518586355312322629)
XLA Ops:
  8.3 7.7 collective-permute-start
  16.0 10.4 collective-permute-done
  26.5 3.6 collective-permute-start.1
  31.9 14.4 %collective-permute-done.1 = bf16[1,2,256,512]{3,2,1,0:T(8,128)(2,1)S(1)} collective-permute-done((bf16[1,2,256,512]{3,2,1,0:T(8,128)(2,1)S(1)}, bf16[1,2,256,512]{3,2,1,0:T(8,128)(2,1)S(1)}, u32[]{:S(2)}, u32[]{:S(2)}) %collective-permute-start.1) | collective-permute-done | bytes 524320 | tf_op jit(solution)/shard_map/ppermute | solution.py:16
  46.4 12.6 %collective-permute-start.2 = (bf16[1,2,256,512]{3,2,1,0:T(8,128)(2,1)S(1)}, bf16[1,2,256,512]{3,2,1,0:T(8,128)(2,1)S(1)}, u32[]{:S(2)}, u32[]{:S(2)}) collective-permute-start(bf16[1,2,256,512]{3,2,1,0:T(8,128)(2,1)S(1)} %broadcast_select_fusion.11), channel_id=1, source_target_pairs={{0,30},{1,31},{2,0},{3,1},{4,2},{5,3},{6,4},{7,5},{8,6},{9,7},{10,... | collective-permute-start | bytes 1572872 | tf_op jit(solution)/shard_map/ppermute | solution.py:16
  59.0 13.9 %collective-permute-done.2 = bf16[1,2,256,512]{3,2,1,0:T(8,128)(2,1)S(1)} collective-permute-done((bf16[1,2,256,512]{3,2,1,0:T(8,128)(2,1)S(1)}, bf16[1,2,256,512]{3,2,1,0:T(8,128)(2,1)S(1)}, u32[]{:S(2)}, u32[]{:S(2)}) %collective-permute-start.2) | collective-permute-done | bytes 524320 | tf_op jit(solution)/shard_map/ppermute | solution.py:16
  73.0 8.3 collective-permute-start.3
  81.3 22.1 %collective-permute-done.3 = bf16[1,2,256,512]{3,2,1,0:T(8,128)(2,1)S(1)} collective-permute-done((bf16[1,2,256,512]{3,2,1,0:T(8,128)(2,1)S(1)}, bf16[1,2,256,512]{3,2,1,0:T(8,128)(2,1)S(1)}, u32[]{:S(2)}, u32[]{:S(2)}) %collective-permute-start.3) | collective-permute-done | bytes 524320 | tf_op jit(solution)/shard_map/ppermute | solution.py:16
  103.4 1.9 collective-permute-start.4
  105.3 12.9 %collective-permute-done.4 = bf16[1,2,256,512]{3,2,1,0:T(8,128)(2,1)S(1)} collective-permute-done((bf16[1,2,256,512]{3,2,1,0:T(8,128)(2,1)S(1)}, bf16[1,2,256,512]{3,2,1,0:T(8,128)(2,1)S(1)}, u32[]{:S(2)}, u32[]{:S(2)}) %collective-permute-start.4) | collective-permute-done | bytes 524320 | tf_op jit(solution)/shard_map/ppermute | solution.py:16
  118.3 1.9 collective-permute-start.5
  120.2 13.4 %collective-permute-done.5 = bf16[1,2,256,512]{3,2,1,0:T(8,128)(2,1)S(1)} collective-permute-done((bf16[1,2,256,512]{3,2,1,0:T(8,128)(2,1)S(1)}, bf16[1,2,256,512]{3,2,1,0:T(8,128)(2,1)S(1)}, u32[]{:S(2)}, u32[]{:S(2)}) %collective-permute-start.5) | collective-permute-done | bytes 524320 | tf_op jit(solution)/shard_map/ppermute | solution.py:16
  133.7 4.3 collective-permute-start.6
  138.0 12.9 %collective-permute-done.6 = bf16[1,2,256,512]{3,2,1,0:T(8,128)(2,1)S(1)} collective-permute-done((bf16[1,2,256,512]{3,2,1,0:T(8,128)(2,1)S(1)}, bf16[1,2,256,512]{3,2,1,0:T(8,128)(2,1)S(1)}, u32[]{:S(2)}, u32[]{:S(2)}) %collective-permute-start.6) | collective-permute-done | bytes 524320 | tf_op jit(solution)/shard_map/ppermute | solution.py:16
  151.4 1.2 fusion.133
  153.9 1.2 fusion.28
  157.6 127.5 %all-gather.5.cloned.1.call-done = f32[32,2,256,256]{3,2,1,0:T(8,128)} async-done(((f32[1,2,256,256]{3,2,1,0:T(8,128)}), f32[32,2,256,256]{3,2,1,0:T(8,128)}) %all-gather.5.cloned.1.call-update) | async-done | bytes 16777232 | tf_op jit(solution)/shard_map/all_gather | solution.py:96
  285.1 6.9 reduce.22
  312.8 2.1 collective-permute-start.7
  314.9 15.1 %collective-permute-done.7 = bf16[1,2,256,512]{3,2,1,0:T(8,128)(2,1)S(1)} collective-permute-done((bf16[1,2,256,512]{3,2,1,0:T(8,128)(2,1)S(1)}, bf16[1,2,256,512]{3,2,1,0:T(8,128)(2,1)S(1)}, u32[]{:S(2)}, u32[]{:S(2)}) %collective-permute-start.7) | collective-permute-done | bytes 524320 | tf_op jit(solution)/shard_map/ppermute | solution.py:16
  330.1 3.0 collective-permute-start.8
  333.1 11.9 %collective-permute-done.8 = bf16[1,2,256,512]{3,2,1,0:T(8,128)(2,1)S(1)} collective-permute-done((bf16[1,2,256,512]{3,2,1,0:T(8,128)(2,1)S(1)}, bf16[1,2,256,512]{3,2,1,0:T(8,128)(2,1)S(1)}, u32[]{:S(2)}, u32[]{:S(2)}) %collective-permute-start.8) | collective-permute-done | bytes 524320 | tf_op jit(solution)/shard_map/ppermute | solution.py:16
  345.1 7.5 collective-permute-start.9
  352.6 19.8 %collective-permute-done.9 = bf16[1,2,256,512]{3,2,1,0:T(8,128)(2,1)S(1)} collective-permute-done((bf16[1,2,256,512]{3,2,1,0:T(8,128)(2,1)S(1)}, bf16[1,2,256,512]{3,2,1,0:T(8,128)(2,1)S(1)}, u32[]{:S(2)}, u32[]{:S(2)}) %collective-permute-start.9) | collective-permute-done | bytes 524320 | tf_op jit(solution)/shard_map/ppermute | solution.py:16
  372.4 3.9 collective-permute-start.10
  376.4 15.1 %collective-permute-done.10 = bf16[1,2,256,512]{3,2,1,0:T(8,128)(2,1)S(1)} collective-permute-done((bf16[1,2,256,512]{3,2,1,0:T(8,128)(2,1)S(1)}, bf16[1,2,256,512]{3,2,1,0:T(8,128)(2,1)S(1)}, u32[]{:S(2)}, u32[]{:S(2)}) %collective-permute-start.10) | collective-permute-done | bytes 524320 | tf_op jit(solution)/shard_map/ppermute | solution.py:16
  391.6 6.7 collective-permute-start.11
  398.2 9.8 collective-permute-done.11
  408.1 4.1 collective-permute-start.12
  412.3 10.4 collective-permute-done.12
  422.7 5.1 collective-permute-start.13
  428.6 18.9 %collective-permute-done.13 = bf16[1,2,256,512]{3,2,1,0:T(8,128)(2,1)S(1)} collective-permute-done((bf16[1,2,256,512]{3,2,1,0:T(8,128)(2,1)S(1)}, bf16[1,2,256,512]{3,2,1,0:T(8,128)(2,1)S(1)}, u32[]{:S(2)}, u32[]{:S(2)}) %collective-permute-start.13) | collective-permute-done | bytes 524320 | tf_op jit(solution)/shard_map/ppermute | solution.py:16
  449.0 104.8 %psum.14 = f32[]{:T(128)} all-reduce(f32[]{:T(128)} %get-tuple-element.10), channel_id=1, replica_groups=mesh['kstr'=16,'pw'=32] {'kstr','pw'}, use_global_device_ids=true, to_apply=%region_6.7 | all-reduce | flops 1 | bytes 8 | tf_op jit(solution)/shard_map/psum | solution.py:113
  554.8 3.1 collective-permute-start.14
  557.9 11.6 %collective-permute-done.14 = bf16[1,2,256,512]{3,2,1,0:T(8,128)(2,1)S(1)} collective-permute-done((bf16[1,2,256,512]{3,2,1,0:T(8,128)(2,1)S(1)}, bf16[1,2,256,512]{3,2,1,0:T(8,128)(2,1)S(1)}, u32[]{:S(2)}, u32[]{:S(2)}) %collective-permute-start.14) | collective-permute-done | bytes 524320 | tf_op jit(solution)/shard_map/ppermute | solution.py:16
  569.5 3.4 collective-permute-start.15
  573.0 8.3 collective-permute-done.15
  581.3 7.2 collective-permute-start.16
  588.5 11.7 %collective-permute-done.16 = bf16[1,2,256,512]{3,2,1,0:T(8,128)(2,1)S(1)} collective-permute-done((bf16[1,2,256,512]{3,2,1,0:T(8,128)(2,1)S(1)}, bf16[1,2,256,512]{3,2,1,0:T(8,128)(2,1)S(1)}, u32[]{:S(2)}, u32[]{:S(2)}) %collective-permute-start.16) | collective-permute-done | bytes 524320 | tf_op jit(solution)/shard_map/ppermute | solution.py:16
  600.2 5.5 collective-permute-start.17
  605.7 21.5 %collective-permute-done.17 = bf16[1,2,256,512]{3,2,1,0:T(8,128)(2,1)S(1)} collective-permute-done((bf16[1,2,256,512]{3,2,1,0:T(8,128)(2,1)S(1)}, bf16[1,2,256,512]{3,2,1,0:T(8,128)(2,1)S(1)}, u32[]{:S(2)}, u32[]{:S(2)}) %collective-permute-start.17) | collective-permute-done | bytes 524320 | tf_op jit(solution)/shard_map/ppermute | solution.py:16
  627.2 3.4 collective-permute-start.18
  630.6 13.5 %collective-permute-done.18 = bf16[1,2,256,512]{3,2,1,0:T(8,128)(2,1)S(1)} collective-permute-done((bf16[1,2,256,512]{3,2,1,0:T(8,128)(2,1)S(1)}, bf16[1,2,256,512]{3,2,1,0:T(8,128)(2,1)S(1)}, u32[]{:S(2)}, u32[]{:S(2)}) %collective-permute-start.18) | collective-permute-done | bytes 524320 | tf_op jit(solution)/shard_map/ppermute | solution.py:16
  644.2 1.9 collective-permute-start.19
  646.1 14.2 %collective-permute-done.19 = bf16[1,2,256,512]{3,2,1,0:T(8,128)(2,1)S(1)} collective-permute-done((bf16[1,2,256,512]{3,2,1,0:T(8,128)(2,1)S(1)}, bf16[1,2,256,512]{3,2,1,0:T(8,128)(2,1)S(1)}, u32[]{:S(2)}, u32[]{:S(2)}) %collective-permute-start.19) | collective-permute-done | bytes 524320 | tf_op jit(solution)/shard_map/ppermute | solution.py:16
  660.4 3.9 collective-permute-start.20
  664.3 7.5 collective-permute-done.20
  674.3 142.4 %all-gather.7.cloned.1.call-done = f32[32,2,256,256]{3,2,1,0:T(8,128)} async-done(((f32[1,2,256,256]{3,2,1,0:T(8,128)}), f32[32,2,256,256]{3,2,1,0:T(8,128)}) %all-gather.7.cloned.1.call-update) | async-done | bytes 16777232 | tf_op jit(solution)/shard_map/all_gather | solution.py:96
  816.7 6.9 reduce.23
  844.3 2.2 collective-permute-start.21
  846.5 15.1 %collective-permute-done.21 = bf16[1,2,256,512]{3,2,1,0:T(8,128)(2,1)S(1)} collective-permute-done((bf16[1,2,256,512]{3,2,1,0:T(8,128)(2,1)S(1)}, bf16[1,2,256,512]{3,2,1,0:T(8,128)(2,1)S(1)}, u32[]{:S(2)}, u32[]{:S(2)}) %collective-permute-start.21) | collective-permute-done | bytes 524320 | tf_op jit(solution)/shard_map/ppermute | solution.py:16
  861.6 3.0 collective-permute-start.22
  864.5 12.0 %collective-permute-done.22 = bf16[1,2,256,512]{3,2,1,0:T(8,128)(2,1)S(1)} collective-permute-done((bf16[1,2,256,512]{3,2,1,0:T(8,128)(2,1)S(1)}, bf16[1,2,256,512]{3,2,1,0:T(8,128)(2,1)S(1)}, u32[]{:S(2)}, u32[]{:S(2)}) %collective-permute-start.22) | collective-permute-done | bytes 524320 | tf_op jit(solution)/shard_map/ppermute | solution.py:16
  876.6 7.5 collective-permute-start.23
  884.1 19.8 %collective-permute-done.23 = bf16[1,2,256,512]{3,2,1,0:T(8,128)(2,1)S(1)} collective-permute-done((bf16[1,2,256,512]{3,2,1,0:T(8,128)(2,1)S(1)}, bf16[1,2,256,512]{3,2,1,0:T(8,128)(2,1)S(1)}, u32[]{:S(2)}, u32[]{:S(2)}) %collective-permute-start.23) | collective-permute-done | bytes 524320 | tf_op jit(solution)/shard_map/ppermute | solution.py:16
  904.0 4.0 collective-permute-start.24
  908.0 15.0 %collective-permute-done.24 = bf16[1,2,256,512]{3,2,1,0:T(8,128)(2,1)S(1)} collective-permute-done((bf16[1,2,256,512]{3,2,1,0:T(8,128)(2,1)S(1)}, bf16[1,2,256,512]{3,2,1,0:T(8,128)(2,1)S(1)}, u32[]{:S(2)}, u32[]{:S(2)}) %collective-permute-start.24) | collective-permute-done | bytes 524320 | tf_op jit(solution)/shard_map/ppermute | solution.py:16
  923.1 6.7 collective-permute-start.25
  929.7 9.8 collective-permute-done.25
  939.6 4.1 collective-permute-start.26
  943.8 10.4 collective-permute-done.26
  954.2 5.1 collective-permute-start.27
  960.1 18.9 %collective-permute-done.27 = bf16[1,2,256,512]{3,2,1,0:T(8,128)(2,1)S(1)} collective-permute-done((bf16[1,2,256,512]{3,2,1,0:T(8,128)(2,1)S(1)}, bf16[1,2,256,512]{3,2,1,0:T(8,128)(2,1)S(1)}, u32[]{:S(2)}, u32[]{:S(2)}) %collective-permute-start.27) | collective-permute-done | bytes 524320 | tf_op jit(solution)/shard_map/ppermute | solution.py:16
  980.5 104.7 %psum.15 = f32[]{:T(128)} all-reduce(f32[]{:T(128)} %get-tuple-element.12), channel_id=1, replica_groups=mesh['kstr'=16,'pw'=32] {'kstr','pw'}, use_global_device_ids=true, to_apply=%region_13.14 | all-reduce | flops 1 | bytes 8 | tf_op jit(solution)/shard_map/psum | solution.py:113
  (149 shorter events, 54.4 us)
Async XLA Ops:
  7.2 277.9 %all-gather.5.cloned.1.call-start = ((), (), s32[]{:S(2)}) async-start(), calls=%async_computation | async-start | bytes 17301504 | tf_op jit(solution)/shard_map/all_gather | solution.py:96
  8.3 18.2 %collective-permute-start = (bf16[1,2,256,512]{3,2,1,0:T(8,128)(2,1)S(1)}, bf16[1,2,256,512]{3,2,1,0:T(8,128)(2,1)S(1)}, u32[]{:S(2)}, u32[]{:S(2)}) collective-permute-start(bf16[1,2,256,512]{3,2,1,0:T(8,128)(2,1)S(1)} %pad_maximum_fusion), channel_id=1, source_target_pairs={{0,480},{32,0},{64,32},{96,64},{128,96},{160,128},{192,160},{224,1... | collective-permute-start | bytes 1572872 | tf_op jit(solution)/shard_map/ppermute | solution.py:16
  26.5 19.8 %collective-permute-start.1 = (bf16[1,2,256,512]{3,2,1,0:T(8,128)(2,1)S(1)}, bf16[1,2,256,512]{3,2,1,0:T(8,128)(2,1)S(1)}, u32[]{:S(2)}, u32[]{:S(2)}) collective-permute-start(bf16[1,2,256,512]{3,2,1,0:T(8,128)(2,1)S(1)} %collective-permute-done), channel_id=1, source_target_pairs={{0,31},{1,0},{2,1},{3,2},{4,3},{5,4},{6,5},{7,6},{8,7},{9,8},{10,9... | collective-permute-start | bytes 1572872 | tf_op jit(solution)/shard_map/ppermute | solution.py:16
  46.4 26.5 %collective-permute-start.2 = (bf16[1,2,256,512]{3,2,1,0:T(8,128)(2,1)S(1)}, bf16[1,2,256,512]{3,2,1,0:T(8,128)(2,1)S(1)}, u32[]{:S(2)}, u32[]{:S(2)}) collective-permute-start(bf16[1,2,256,512]{3,2,1,0:T(8,128)(2,1)S(1)} %broadcast_select_fusion.11), channel_id=1, source_target_pairs={{0,30},{1,31},{2,0},{3,1},{4,2},{5,3},{6,4},{7,5},{8,6},{9,7},{10,... | collective-permute-start | bytes 1572872 | tf_op jit(solution)/shard_map/ppermute | solution.py:16
  73.0 30.4 %collective-permute-start.3 = (bf16[1,2,256,512]{3,2,1,0:T(8,128)(2,1)S(1)}, bf16[1,2,256,512]{3,2,1,0:T(8,128)(2,1)S(1)}, u32[]{:S(2)}, u32[]{:S(2)}) collective-permute-start(bf16[1,2,256,512]{3,2,1,0:T(8,128)(2,1)S(1)} %broadcast_select_fusion.13), channel_id=1, source_target_pairs={{0,28},{1,29},{2,30},{3,31},{4,0},{5,1},{6,2},{7,3},{8,4},{9,5},{1... | collective-permute-start | bytes 1572872 | tf_op jit(solution)/shard_map/ppermute | solution.py:16
  103.4 14.8 %collective-permute-start.4 = (bf16[1,2,256,512]{3,2,1,0:T(8,128)(2,1)S(1)}, bf16[1,2,256,512]{3,2,1,0:T(8,128)(2,1)S(1)}, u32[]{:S(2)}, u32[]{:S(2)}) collective-permute-start(bf16[1,2,256,512]{3,2,1,0:T(8,128)(2,1)S(1)} %broadcast_select_fusion.15), channel_id=1, source_target_pairs={{0,24},{1,25},{2,26},{3,27},{4,28},{5,29},{6,30},{7,31},{8,0},{9,1... | collective-permute-start | bytes 1572872 | tf_op jit(solution)/shard_map/ppermute | solution.py:16
  118.3 15.4 %collective-permute-start.5 = (bf16[1,2,256,512]{3,2,1,0:T(8,128)(2,1)S(1)}, bf16[1,2,256,512]{3,2,1,0:T(8,128)(2,1)S(1)}, u32[]{:S(2)}, u32[]{:S(2)}) collective-permute-start(bf16[1,2,256,512]{3,2,1,0:T(8,128)(2,1)S(1)} %broadcast_select_fusion.17), channel_id=1, source_target_pairs={{0,16},{1,17},{2,18},{3,19},{4,20},{5,21},{6,22},{7,23},{8,24},{9,... | collective-permute-start | bytes 1572872 | tf_op jit(solution)/shard_map/ppermute | solution.py:16
  133.7 17.2 %collective-permute-start.6 = (bf16[1,2,256,512]{3,2,1,0:T(8,128)(2,1)S(1)}, bf16[1,2,256,512]{3,2,1,0:T(8,128)(2,1)S(1)}, u32[]{:S(2)}, u32[]{:S(2)}) collective-permute-start(bf16[1,2,256,512]{3,2,1,0:T(8,128)(2,1)S(1)} %broadcast_select_fusion.19), channel_id=1, source_target_pairs={{0,31},{1,0},{2,1},{3,2},{4,3},{5,4},{6,5},{7,6},{8,7},{9,8},{10,9... | collective-permute-start | bytes 1572872 | tf_op jit(solution)/shard_map/ppermute | solution.py:16
  157.4 659.3 %all-gather.7.cloned.1.call-start = ((), (), s32[]{:S(2)}) async-start(), calls=%async_computation.1 | async-start | bytes 17301504 | tf_op jit(solution)/shard_map/all_gather | solution.py:96
  298.2 13.5 %copy-start.1 = (bf16[1,256,512]{2,1,0:T(8,128)(2,1)S(1)}, bf16[1,256,512]{2,1,0:T(8,128)(2,1)}, u32[]{:S(2)}) copy-start(bf16[1,256,512]{2,1,0:T(8,128)(2,1)} %param.3) | copy-start | bytes 786436
  298.6 13.3 %copy-start = (bf16[1,256,512]{2,1,0:T(8,128)(2,1)S(1)}, bf16[1,256,512]{2,1,0:T(8,128)(2,1)}, u32[]{:S(2)}) copy-start(bf16[1,256,512]{2,1,0:T(8,128)(2,1)} %param.4) | copy-start | bytes 786436
  312.8 17.3 %collective-permute-start.7 = (bf16[1,2,256,512]{3,2,1,0:T(8,128)(2,1)S(1)}, bf16[1,2,256,512]{3,2,1,0:T(8,128)(2,1)S(1)}, u32[]{:S(2)}, u32[]{:S(2)}) collective-permute-start(bf16[1,2,256,512]{3,2,1,0:T(8,128)(2,1)S(1)} %pad_maximum_fusion.2), channel_id=1, source_target_pairs={{0,32},{32,64},{64,96},{96,128},{128,160},{160,192},{192,224},{224... | collective-permute-start | bytes 1572872 | tf_op jit(solution)/shard_map/ppermute | solution.py:16
  330.1 14.9 %collective-permute-start.8 = (bf16[1,2,256,512]{3,2,1,0:T(8,128)(2,1)S(1)}, bf16[1,2,256,512]{3,2,1,0:T(8,128)(2,1)S(1)}, u32[]{:S(2)}, u32[]{:S(2)}) collective-permute-start(bf16[1,2,256,512]{3,2,1,0:T(8,128)(2,1)S(1)} %collective-permute-done.7), channel_id=1, source_target_pairs={{0,31},{1,0},{2,1},{3,2},{4,3},{5,4},{6,5},{7,6},{8,7},{9,8},{10,9... | collective-permute-start | bytes 1572872 | tf_op jit(solution)/shard_map/ppermute | solution.py:16
  345.1 27.3 %collective-permute-start.9 = (bf16[1,2,256,512]{3,2,1,0:T(8,128)(2,1)S(1)}, bf16[1,2,256,512]{3,2,1,0:T(8,128)(2,1)S(1)}, u32[]{:S(2)}, u32[]{:S(2)}) collective-permute-start(bf16[1,2,256,512]{3,2,1,0:T(8,128)(2,1)S(1)} %broadcast_select_fusion.1), channel_id=1, source_target_pairs={{0,30},{1,31},{2,0},{3,1},{4,2},{5,3},{6,4},{7,5},{8,6},{9,7},{10,... | collective-permute-start | bytes 1572872 | tf_op jit(solution)/shard_map/ppermute | solution.py:16
  372.4 19.0 %collective-permute-start.10 = (bf16[1,2,256,512]{3,2,1,0:T(8,128)(2,1)S(1)}, bf16[1,2,256,512]{3,2,1,0:T(8,128)(2,1)S(1)}, u32[]{:S(2)}, u32[]{:S(2)}) collective-permute-start(bf16[1,2,256,512]{3,2,1,0:T(8,128)(2,1)S(1)} %broadcast_select_fusion.3), channel_id=1, source_target_pairs={{0,28},{1,29},{2,30},{3,31},{4,0},{5,1},{6,2},{7,3},{8,4},{9,5},{1... | collective-permute-start | bytes 1572872 | tf_op jit(solution)/shard_map/ppermute | solution.py:16
  391.6 16.5 %collective-permute-start.11 = (bf16[1,2,256,512]{3,2,1,0:T(8,128)(2,1)S(1)}, bf16[1,2,256,512]{3,2,1,0:T(8,128)(2,1)S(1)}, u32[]{:S(2)}, u32[]{:S(2)}) collective-permute-start(bf16[1,2,256,512]{3,2,1,0:T(8,128)(2,1)S(1)} %broadcast_select_fusion.5), channel_id=1, source_target_pairs={{0,24},{1,25},{2,26},{3,27},{4,28},{5,29},{6,30},{7,31},{8,0},{9,1... | collective-permute-start | bytes 1572872 | tf_op jit(solution)/shard_map/ppermute | solution.py:16
  408.1 14.5 %collective-permute-start.12 = (bf16[1,2,256,512]{3,2,1,0:T(8,128)(2,1)S(1)}, bf16[1,2,256,512]{3,2,1,0:T(8,128)(2,1)S(1)}, u32[]{:S(2)}, u32[]{:S(2)}) collective-permute-start(bf16[1,2,256,512]{3,2,1,0:T(8,128)(2,1)S(1)} %broadcast_select_fusion.7), channel_id=1, source_target_pairs={{0,16},{1,17},{2,18},{3,19},{4,20},{5,21},{6,22},{7,23},{8,24},{9,... | collective-permute-start | bytes 1572872 | tf_op jit(solution)/shard_map/ppermute | solution.py:16
  422.7 24.8 %collective-permute-start.13 = (bf16[1,2,256,512]{3,2,1,0:T(8,128)(2,1)S(1)}, bf16[1,2,256,512]{3,2,1,0:T(8,128)(2,1)S(1)}, u32[]{:S(2)}, u32[]{:S(2)}) collective-permute-start(bf16[1,2,256,512]{3,2,1,0:T(8,128)(2,1)S(1)} %broadcast_select_fusion.9), channel_id=1, source_target_pairs={{0,31},{1,0},{2,1},{3,2},{4,3},{5,4},{6,5},{7,6},{8,7},{9,8},{10,9... | collective-permute-start | bytes 1572872 | tf_op jit(solution)/shard_map/ppermute | solution.py:16
  554.8 14.7 %collective-permute-start.14 = (bf16[1,2,256,512]{3,2,1,0:T(8,128)(2,1)S(1)}, bf16[1,2,256,512]{3,2,1,0:T(8,128)(2,1)S(1)}, u32[]{:S(2)}, u32[]{:S(2)}) collective-permute-start(bf16[1,2,256,512]{3,2,1,0:T(8,128)(2,1)S(1)} %pad_maximum_fusion.3), channel_id=1, source_target_pairs={{0,480},{32,0},{64,32},{96,64},{128,96},{160,128},{192,160},{224,1... | collective-permute-start | bytes 1572872 | tf_op jit(solution)/shard_map/ppermute | solution.py:16
  569.5 11.7 %collective-permute-start.15 = (bf16[1,2,256,512]{3,2,1,0:T(8,128)(2,1)S(1)}, bf16[1,2,256,512]{3,2,1,0:T(8,128)(2,1)S(1)}, u32[]{:S(2)}, u32[]{:S(2)}) collective-permute-start(bf16[1,2,256,512]{3,2,1,0:T(8,128)(2,1)S(1)} %collective-permute-done.14), channel_id=1, source_target_pairs={{0,31},{1,0},{2,1},{3,2},{4,3},{5,4},{6,5},{7,6},{8,7},{9,8},{10,9... | collective-permute-start | bytes 1572872 | tf_op jit(solution)/shard_map/ppermute | solution.py:16
  581.3 18.8 %collective-permute-start.16 = (bf16[1,2,256,512]{3,2,1,0:T(8,128)(2,1)S(1)}, bf16[1,2,256,512]{3,2,1,0:T(8,128)(2,1)S(1)}, u32[]{:S(2)}, u32[]{:S(2)}) collective-permute-start(bf16[1,2,256,512]{3,2,1,0:T(8,128)(2,1)S(1)} %broadcast_select_fusion.10), channel_id=1, source_target_pairs={{0,30},{1,31},{2,0},{3,1},{4,2},{5,3},{6,4},{7,5},{8,6},{9,7},{10,... | collective-permute-start | bytes 1572872 | tf_op jit(solution)/shard_map/ppermute | solution.py:16
  600.2 27.0 %collective-permute-start.17 = (bf16[1,2,256,512]{3,2,1,0:T(8,128)(2,1)S(1)}, bf16[1,2,256,512]{3,2,1,0:T(8,128)(2,1)S(1)}, u32[]{:S(2)}, u32[]{:S(2)}) collective-permute-start(bf16[1,2,256,512]{3,2,1,0:T(8,128)(2,1)S(1)} %broadcast_select_fusion.12), channel_id=1, source_target_pairs={{0,28},{1,29},{2,30},{3,31},{4,0},{5,1},{6,2},{7,3},{8,4},{9,5},{1... | collective-permute-start | bytes 1572872 | tf_op jit(solution)/shard_map/ppermute | solution.py:16
  627.2 16.9 %collective-permute-start.18 = (bf16[1,2,256,512]{3,2,1,0:T(8,128)(2,1)S(1)}, bf16[1,2,256,512]{3,2,1,0:T(8,128)(2,1)S(1)}, u32[]{:S(2)}, u32[]{:S(2)}) collective-permute-start(bf16[1,2,256,512]{3,2,1,0:T(8,128)(2,1)S(1)} %broadcast_select_fusion.14), channel_id=1, source_target_pairs={{0,24},{1,25},{2,26},{3,27},{4,28},{5,29},{6,30},{7,31},{8,0},{9,1... | collective-permute-start | bytes 1572872 | tf_op jit(solution)/shard_map/ppermute | solution.py:16
  644.2 16.2 %collective-permute-start.19 = (bf16[1,2,256,512]{3,2,1,0:T(8,128)(2,1)S(1)}, bf16[1,2,256,512]{3,2,1,0:T(8,128)(2,1)S(1)}, u32[]{:S(2)}, u32[]{:S(2)}) collective-permute-start(bf16[1,2,256,512]{3,2,1,0:T(8,128)(2,1)S(1)} %broadcast_select_fusion.16), channel_id=1, source_target_pairs={{0,16},{1,17},{2,18},{3,19},{4,20},{5,21},{6,22},{7,23},{8,24},{9,... | collective-permute-start | bytes 1572872 | tf_op jit(solution)/shard_map/ppermute | solution.py:16
  660.4 11.4 %collective-permute-start.20 = (bf16[1,2,256,512]{3,2,1,0:T(8,128)(2,1)S(1)}, bf16[1,2,256,512]{3,2,1,0:T(8,128)(2,1)S(1)}, u32[]{:S(2)}, u32[]{:S(2)}) collective-permute-start(bf16[1,2,256,512]{3,2,1,0:T(8,128)(2,1)S(1)} %broadcast_select_fusion.18), channel_id=1, source_target_pairs={{0,31},{1,0},{2,1},{3,2},{4,3},{5,4},{6,5},{7,6},{8,7},{9,8},{10,9... | collective-permute-start | bytes 1572872 | tf_op jit(solution)/shard_map/ppermute | solution.py:16
  844.3 17.3 %collective-permute-start.21 = (bf16[1,2,256,512]{3,2,1,0:T(8,128)(2,1)S(1)}, bf16[1,2,256,512]{3,2,1,0:T(8,128)(2,1)S(1)}, u32[]{:S(2)}, u32[]{:S(2)}) collective-permute-start(bf16[1,2,256,512]{3,2,1,0:T(8,128)(2,1)S(1)} %pad_maximum_fusion.5), channel_id=1, source_target_pairs={{0,32},{32,64},{64,96},{96,128},{128,160},{160,192},{192,224},{224... | collective-permute-start | bytes 1572872 | tf_op jit(solution)/shard_map/ppermute | solution.py:16
  861.6 15.0 %collective-permute-start.22 = (bf16[1,2,256,512]{3,2,1,0:T(8,128)(2,1)S(1)}, bf16[1,2,256,512]{3,2,1,0:T(8,128)(2,1)S(1)}, u32[]{:S(2)}, u32[]{:S(2)}) collective-permute-start(bf16[1,2,256,512]{3,2,1,0:T(8,128)(2,1)S(1)} %collective-permute-done.21), channel_id=1, source_target_pairs={{0,31},{1,0},{2,1},{3,2},{4,3},{5,4},{6,5},{7,6},{8,7},{9,8},{10,9... | collective-permute-start | bytes 1572872 | tf_op jit(solution)/shard_map/ppermute | solution.py:16
  876.6 27.3 %collective-permute-start.23 = (bf16[1,2,256,512]{3,2,1,0:T(8,128)(2,1)S(1)}, bf16[1,2,256,512]{3,2,1,0:T(8,128)(2,1)S(1)}, u32[]{:S(2)}, u32[]{:S(2)}) collective-permute-start(bf16[1,2,256,512]{3,2,1,0:T(8,128)(2,1)S(1)} %broadcast_select_fusion), channel_id=1, source_target_pairs={{0,30},{1,31},{2,0},{3,1},{4,2},{5,3},{6,4},{7,5},{8,6},{9,7},{10,... | collective-permute-start | bytes 1572872 | tf_op jit(solution)/shard_map/ppermute | solution.py:16
  904.0 19.0 %collective-permute-start.24 = (bf16[1,2,256,512]{3,2,1,0:T(8,128)(2,1)S(1)}, bf16[1,2,256,512]{3,2,1,0:T(8,128)(2,1)S(1)}, u32[]{:S(2)}, u32[]{:S(2)}) collective-permute-start(bf16[1,2,256,512]{3,2,1,0:T(8,128)(2,1)S(1)} %broadcast_select_fusion.2), channel_id=1, source_target_pairs={{0,28},{1,29},{2,30},{3,31},{4,0},{5,1},{6,2},{7,3},{8,4},{9,5},{1... | collective-permute-start | bytes 1572872 | tf_op jit(solution)/shard_map/ppermute | solution.py:16
  923.1 16.5 %collective-permute-start.25 = (bf16[1,2,256,512]{3,2,1,0:T(8,128)(2,1)S(1)}, bf16[1,2,256,512]{3,2,1,0:T(8,128)(2,1)S(1)}, u32[]{:S(2)}, u32[]{:S(2)}) collective-permute-start(bf16[1,2,256,512]{3,2,1,0:T(8,128)(2,1)S(1)} %broadcast_select_fusion.4), channel_id=1, source_target_pairs={{0,24},{1,25},{2,26},{3,27},{4,28},{5,29},{6,30},{7,31},{8,0},{9,1... | collective-permute-start | bytes 1572872 | tf_op jit(solution)/shard_map/ppermute | solution.py:16
  939.6 14.5 %collective-permute-start.26 = (bf16[1,2,256,512]{3,2,1,0:T(8,128)(2,1)S(1)}, bf16[1,2,256,512]{3,2,1,0:T(8,128)(2,1)S(1)}, u32[]{:S(2)}, u32[]{:S(2)}) collective-permute-start(bf16[1,2,256,512]{3,2,1,0:T(8,128)(2,1)S(1)} %broadcast_select_fusion.6), channel_id=1, source_target_pairs={{0,16},{1,17},{2,18},{3,19},{4,20},{5,21},{6,22},{7,23},{8,24},{9,... | collective-permute-start | bytes 1572872 | tf_op jit(solution)/shard_map/ppermute | solution.py:16
  954.2 24.8 %collective-permute-start.27 = (bf16[1,2,256,512]{3,2,1,0:T(8,128)(2,1)S(1)}, bf16[1,2,256,512]{3,2,1,0:T(8,128)(2,1)S(1)}, u32[]{:S(2)}, u32[]{:S(2)}) collective-permute-start(bf16[1,2,256,512]{3,2,1,0:T(8,128)(2,1)S(1)} %broadcast_select_fusion.8), channel_id=1, source_target_pairs={{0,31},{1,0},{2,1},{3,2},{4,3},{5,4},{6,5},{7,6},{8,7},{9,8},{10,9... | collective-permute-start | bytes 1572872 | tf_op jit(solution)/shard_map/ppermute | solution.py:16
Sparse Core Ops, SparseCore 0:
  157.5 127.5 all-gather.4
  674.4 142.2 all-gather.6
